TPU v7x, 32 devices: a whole 2x2x4 slice. The times are simulated.
32 devices in a mesh: member: 2 (over y), gx: 8 (over z, x), gy: 2 (over core).
Axes of the slice: x: 2, y: 2, z: 4, core: 2. Of those that a mesh axis runs over, the one named last changes fastest.
Arguments:
- conserved: float32 [5, 64, 64, 256], P(None, ('member', 'gx'), 'gy'), parts along dimension 1, may hold values from -3 to 18, as said below
- solid_mask: int32 [64, 64, 256], P(('member', 'gx'), 'gy'), parts along dimension 0, may hold values 0 or 1
- penalty: float32 [512], P('member'), parts along dimension 0, may hold values from 20 to 400
Outputs:
- advanced: float32 [5, 64, 64, 256], P(None, ('member', 'gx'), 'gy'), parts along dimension 1
There are 2 independent parts, one for each index of `member`. A program takes and returns all parts, laid end to end along the dimension named above; each array names one. Nothing has to cross between parts.
Inputs may be any that keep to these rules, and one draw needn't show every extreme that they name: `conserved`: component 0 (density) lies in 0.8 to 2 and the pressure computed from every cell is positive.
All inputs are finite; a program needn't handle non-finite values. No bound on the sum of `solid_mask` on one device may be relied on, other than what follows from the above.
Results may differ from a plain program's by a relative error of at most 0.00002.
Values sent between devices are 32-bit elements; how exact they have to be, the bound alone decides.
A program may use at most 64 MiB of HBM per device.

v0:
```python
import jax
import jax.numpy as jnp
from jax import lax
from jax.sharding import PartitionSpec as P

GAMMA_LESS = 0.4
GAMMA_FULL = 1.4
COURANT = 0.3
VISCOSITY = 0.05


def extended(block, sides, width):
    for axis, dim in sides:
        count = lax.axis_size(axis)
        forward = [(i, i + 1) for i in range(count - 1)]
        forward.append((count - 1, 0))
        backward = [(target, source) for source, target in forward]
        low = lax.ppermute(
            lax.slice_in_dim(block, block.shape[dim] - width, None, axis=dim), axis, forward
        )
        high = lax.ppermute(lax.slice_in_dim(block, 0, width, axis=dim), axis, backward)
        block = jnp.concatenate([low, block, high], axis=dim)
    return block


def pressure_of(fields):
    mass_per_volume = fields[0]
    squares = fields[1] * fields[1] + fields[2] * fields[2] + fields[3] * fields[3]
    return (GAMMA_LESS * (fields[4] - 0.5 * squares / mass_per_volume), squares)


def speeds(fields):
    normal_stress, squares = pressure_of(fields)
    mass_per_volume = fields[0]
    return jnp.sqrt(squares / mass_per_volume / mass_per_volume) + jnp.sqrt(
        GAMMA_FULL * normal_stress / mass_per_volume
    )


def fluxes(fields, direction):
    mass_per_volume = fields[0]
    normal_stress, squares = pressure_of(fields)
    velocity = fields[1 + direction] / mass_per_volume
    components = [
        fields[1 + direction],
        fields[1] * velocity,
        fields[2] * velocity,
        fields[3] * velocity,
        (fields[4] + normal_stress) * velocity,
    ]
    components[1 + direction] = components[1 + direction] + normal_stress
    return jnp.stack(components)


def axis_slope(values, along, extent):
    first_part = lax.slice_in_dim(values, 0, extent, axis=along)
    second_part = lax.slice_in_dim(values, 1, extent + 1, axis=along)
    fourth_part = lax.slice_in_dim(values, 3, extent + 3, axis=along)
    fifth_part = lax.slice_in_dim(values, 4, extent + 4, axis=along)
    return (first_part - 8.0 * second_part + 8.0 * fourth_part - fifth_part) / 12.0


def axis_curve(values, along, extent):
    first_part = lax.slice_in_dim(values, 0, extent, axis=along)
    second_part = lax.slice_in_dim(values, 1, extent + 1, axis=along)
    middle_part = lax.slice_in_dim(values, 2, extent + 2, axis=along)
    fourth_part = lax.slice_in_dim(values, 3, extent + 3, axis=along)
    fifth_part = lax.slice_in_dim(values, 4, extent + 4, axis=along)
    return (
        -first_part + 16.0 * second_part - 30.0 * middle_part + 16.0 * fourth_part - fifth_part
    ) / 12.0


def roll_slope(values):
    return (
        jnp.roll(values, 2, 3)
        - 8.0 * jnp.roll(values, 1, 3)
        + 8.0 * jnp.roll(values, -1, 3)
        - jnp.roll(values, -2, 3)
    ) / 12.0


def roll_curve(values):
    return (
        -jnp.roll(values, 2, 3)
        + 16.0 * jnp.roll(values, 1, 3)
        - 30.0 * values
        + 16.0 * jnp.roll(values, -1, 3)
        - jnp.roll(values, -2, 3)
    ) / 12.0


def operate(padded):
    extent_x = padded.shape[1] - 4
    extent_y = padded.shape[2] - 4
    inner_cells = padded[:, 2:-2, 2:-2]
    strip_x = padded[:, :, 2:-2]
    strip_y = padded[:, 2:-2, :]
    divergence = axis_slope(fluxes(strip_x, 0), 1, extent_x)
    divergence = divergence + axis_slope(fluxes(strip_y, 1), 2, extent_y)
    divergence = divergence + roll_slope(fluxes(inner_cells, 2))
    diffusion = (
        axis_curve(strip_x[1:], 1, extent_x)
        + axis_curve(strip_y[1:], 2, extent_y)
        + roll_curve(inner_cells[1:])
    )
    return jnp.concatenate([-divergence[:1], -divergence[1:] + VISCOSITY * diffusion], 0)


def damp_momenta(fields, time_step, brinkman):
    return jnp.concatenate([fields[:1], fields[1:4] / (1.0 + time_step * brinkman), fields[4:]], 0)


def extend_rim(fields):
    return extended(fields, (("gx", 1), ("gy", 2)), 2)


def per_device(conserved, solid_mask, penalty):
    brinkman = solid_mask.astype(jnp.float32) * penalty[None, None, :]
    fastest = lax.pmax(jnp.max(speeds(conserved)), ("gx", "gy"))
    time_step = COURANT / fastest
    tendency = operate(extend_rim(conserved))
    section_one = damp_momenta(conserved + time_step * tendency, time_step, brinkman)
    second_tendency = operate(extend_rim(section_one))
    section_two = 0.5 * conserved + 0.5 * (section_one + time_step * second_tendency)
    return damp_momenta(section_two, time_step, brinkman)


def solution(mesh):
    return jax.shard_map(
        per_device,
        mesh=mesh,
        in_specs=(
            P(None, ("member", "gx"), "gy", None),
            P(("member", "gx"), "gy", None),
            P("member"),
        ),
        out_specs=P(None, ("member", "gx"), "gy", None),
        check_vma=False,
    )
```

profile of v0, /device:TPU:0, one launch (start us, length us, event | category | flops | bytes accessed | tf_op | source)
XLA Modules:
  0.0 79.8 jit_solution(14406027075489586206)
XLA Ops:
  0.0 2.0 %fusion.85 = (f32[5,2,32,256]{3,2,1,0:T(8,128)}, f32[5,2,32,256]{3,2,1,0:T(8,128)}) fusion(f32[5,4,32,256]{3,2,1,0:T(8,128)} %param.3), kind=kLoop, calls=%fused_computation.234 | loop fusion | bytes 1310720 | tf_op jit(solution)/shard_map/slice | solution.py:21
  2.1 2.9 %collective-permute-start = (f32[5,2,32,256]{3,2,1,0:T(8,128)}, f32[5,2,32,256]{3,2,1,0:T(8,128)}, u32[]{:S(2)}, u32[]{:S(2)}) collective-permute-start(f32[5,2,32,256]{3,2,1,0:T(8,128)} %get-tuple-element.76), channel_id=1, source_target_pairs={{0,2},{2,4},{4,6},{6,8},{8,10},{10,12},{12,14},{14,0},{1,3},{3,5},... | collective-permute-start | bytes 983048 | tf_op jit(solution)/shard_map/ppermute | solution.py:18
  5.0 3.0 %collective-permute-start.1 = (f32[5,2,32,256]{3,2,1,0:T(8,128)}, f32[5,2,32,256]{3,2,1,0:T(8,128)}, u32[]{:S(2)}, u32[]{:S(2)}) collective-permute-start(f32[5,2,32,256]{3,2,1,0:T(8,128)} %get-tuple-element.75), channel_id=1, source_target_pairs={{2,0},{4,2},{6,4},{8,6},{10,8},{12,10},{14,12},{0,14},{3,1},{5,3},... | collective-permute-start | bytes 983048 | tf_op jit(solution)/shard_map/ppermute | solution.py:21
  8.1 0.1 add_dynamic-update-slice_fusion.5
  8.2 0.2 fusion.81
  8.5 0.9 %fusion.82 = (f32[5,4,32,2]{3,2,1,0:T(8,128)}, f32[5,4,32,2]{3,2,1,0:T(8,128)}) fusion(f32[5,4,32,256]{3,2,1,0:T(8,128)S(1)} %multiply_dynamic-update-slice_fusion.15), kind=kLoop, calls=%fused_computation.231 | loop fusion | bytes 20480 | tf_op jit(solution)/shard_map/jit(_roll_static)/slice | solution.py:79
  9.4 0.2 fusion.83
  9.7 0.9 %fusion.84 = (f32[5,4,32,1]{3,2,1,0:T(8,128)}, f32[5,4,32,1]{3,2,1,0:T(8,128)}) fusion(f32[5,4,32,256]{3,2,1,0:T(8,128)S(1)} %multiply_dynamic-update-slice_fusion.15), kind=kLoop, calls=%fused_computation.233 | loop fusion | bytes 10240 | tf_op jit(solution)/shard_map/jit(_roll_static)/slice | solution.py:78
  10.6 1.1 %fusion.77 = (f32[4,4,32,254]{3,2,1,0:T(8,128)}, f32[4,4,32,254]{3,2,1,0:T(8,128)}) fusion(f32[5,4,32,256]{3,2,1,0:T(8,128)S(1)} %copy-done), kind=kLoop, calls=%fused_computation.226 | loop fusion | bytes 2080768 | tf_op jit(solution)/shard_map/jit(_roll_static)/slice | solution.py:89
  11.7 0.8 %fusion.78 = (f32[4,4,32,2]{3,2,1,0:T(8,128)S(1)}, f32[4,4,32,2]{3,2,1,0:T(8,128)}) fusion(f32[5,4,32,256]{3,2,1,0:T(8,128)S(1)} %copy-done), kind=kLoop, calls=%fused_computation.227 | loop fusion | bytes 16384 | tf_op jit(solution)/shard_map/jit(_roll_static)/slice | solution.py:89
  12.6 1.2 %fusion.79 = (f32[4,4,32,255]{3,2,1,0:T(8,128)}, f32[4,4,32,255]{3,2,1,0:T(8,128)}) fusion(f32[5,4,32,256]{3,2,1,0:T(8,128)S(1)} %copy-done), kind=kLoop, calls=%fused_computation.228 | loop fusion | bytes 2088960 | tf_op jit(solution)/shard_map/jit(_roll_static)/slice | solution.py:88
  13.7 0.8 %fusion.69 = f32[]{:T(128)} fusion(f32[5,4,32,256]{3,2,1,0:T(8,128)S(1)} %copy-done), kind=kLoop, calls=%fused_computation.203 | loop fusion | flops 458751 | bytes 655364 | tf_op jit(solution)/shard_map/reduce_max | solution.py:120
  14.5 0.9 %fusion.80 = (f32[4,4,32,1]{3,2,1,0:T(8,128)}, f32[4,4,32,1]{3,2,1,0:T(8,128)}) fusion(f32[5,4,32,256]{3,2,1,0:T(8,128)S(1)} %copy-done), kind=kLoop, calls=%fused_computation.229 | loop fusion | bytes 8192 | tf_op jit(solution)/shard_map/jit(_roll_static)/slice | solution.py:88
  15.4 31.2 %pmax.7 = f32[]{:T(128)} all-reduce(f32[]{:T(128)} %fusion.69), channel_id=1, replica_groups=mesh['member'=2,'gx'=8,'gy'=2] {'gx','gy'}, use_global_device_ids=true, to_apply=%region_1.0 | all-reduce | flops 1 | bytes 8 | tf_op jit(solution)/shard_map/pmax | solution.py:120
  47.3 0.9 %multiply_add_fusion = f32[4,32,256]{2,1,0:T(8,128)S(1)} fusion(s32[4,32,256]{2,1,0:T(8,128)} %param.4, f32[256]{0:T(256)S(1)} %copy-done.12, f32[]{:T(128)S(6)} %div.138), kind=kLoop, calls=%fused_computation.196 | loop fusion | flops 131072 | bytes 263172 | tf_op jit(solution)/shard_map/add | solution.py:111
  48.3 1.0 %constant_dynamic-update-slice_fusion.5 = (f32[5,6,32,256]{3,2,1,0:T(8,128)S(1)}, f32[5,8,32,256]{3,2,1,0:T(8,128)S(1)}) fusion(f32[5,2,32,256]{3,2,1,0:T(8,128)} %collective-permute-done), kind=kLoop, calls=%fused_computation.215 | loop fusion | bytes 983040
  49.3 0.2 constant_dynamic-update-slice_fusion.4
  49.6 1.0 %constant_dynamic-update-slice_fusion.6 = (f32[5,6,32,256]{3,2,1,0:T(8,128)S(1)}, f32[5,8,32,256]{3,2,1,0:T(8,128)S(1)}) fusion(f32[5,6,32,256]{3,2,1,0:T(8,128)S(1)} %get-tuple-element.73, f32[5,2,32,256]{3,2,1,0:T(8,128)} %collective-permute-done.1, f32[5,8,32,256]{3,2,1,0:T(8,128)S(1)} %get-tuple-element.74), kind=kLoop, calls=%fused_computation.216 | loop fusion | bytes 983040 | tf_op jit(solution)/shard_map/concatenate | solution.py:22
  50.7 0.1 collective-permute-start.3
  50.8 0.5 collective-permute-start.2
  51.3 0.1 add_dynamic-update-slice_fusion.1
  51.6 0.5 collective-permute-done.3
  52.0 0.2 collective-permute-done.2
  52.2 0.1 multiply_dynamic-update-slice_fusion.11
  52.3 0.1 add_dynamic-update-slice_fusion.3
  52.5 0.1 multiply_dynamic-update-slice_fusion.9
  52.6 0.8 copy-done.5
  53.4 0.1 copy-done.6
  53.5 0.1 copy-done.7
  53.6 0.1 copy-done.8
  53.8 0.8 %fusion.9 = f32[5,4,32,256]{3,2,1,0:T(8,128)S(1)} fusion(f32[5,4,36,256]{3,2,1,0:T(8,128)S(1)} %multiply_dynamic-update-slice_fusion.9, f32[5,8,32,256]{3,2,1,0:T(8,128)S(1)} %multiply_dynamic-update-slice_fusion.3, f32[5,4,32,254]{3,2,1,0:T(8,128)S(1)} %get-tuple-element.65, f32[5,4,32,2]{3,2,1,0:T(8,128)S(1)} %copy-done.6, ...), kind=kLoop, calls=%fused_computation.36 | loop fusion | flops 3604480 | bytes 8519680 | tf_op jit(solution)/shard_map/add | solution.py:101
  54.6 0.2 copy-done.1
  54.8 0.2 copy-done.2
  54.9 0.2 copy-done.3
  55.1 0.2 copy-done.4
  55.3 0.1 copy-done.10
  55.4 0.1 copy-done.11
  55.5 0.9 %fusion.46 = f32[4,4,32,256]{3,2,1,0:T(8,128)S(1)} fusion(f32[5,8,2,256]{3,2,1,0:T(2,128)S(1)} %collective-permute-done.3, f32[5,8,32,256]{3,2,1,0:T(8,128)S(1)} %get-tuple-element.88, f32[5,8,2,256]{3,2,1,0:T(2,128)S(1)} %collective-permute-done.2, f32[5,6,32,256]{3,2,1,0:T(8,128)S(1)} %get-tuple-element.87, f32[5,6,32,256]{3,2,1,0:T(8,128)S(1)} %get-tuple-element.72, ...), kind=kLoop, calls=%fused_computation.106 | loop fusion | flops 4587520 | bytes 7241728 | tf_op jit(solution)/shard_map/add | solution.py:107
  56.3 0.1 fusion.16
  56.5 0.1 add_dynamic-update-slice_fusion.4
  56.7 0.2 fusion.72
  56.9 0.2 fusion.73
  57.1 0.2 fusion.75
  57.2 0.2 fusion.25
  57.4 0.1 fusion.62
  57.6 0.2 fusion.24
  58.0 2.0 %collective-permute-start.4 = (f32[5,2,32,256]{3,2,1,0:T(8,128)S(1)}, f32[5,2,32,256]{3,2,1,0:T(8,128)S(1)}, u32[]{:S(2)}, u32[]{:S(2)}) collective-permute-start(f32[5,2,32,256]{3,2,1,0:T(8,128)S(1)} %get-tuple-element.54), channel_id=1, source_target_pairs={{0,2},{2,4},{4,6},{6,8},{8,10},{10,12},{12,14},{14,0},{1,3},{3,5},... | collective-permute-start | bytes 983048 | tf_op jit(solution)/shard_map/ppermute | solution.py:18
  60.0 0.1 fusion.61
  60.2 0.2 fusion.74
  60.4 14.6 %collective-permute-done.5 = f32[5,2,32,256]{3,2,1,0:T(8,128)S(1)} collective-permute-done((f32[5,2,32,256]{3,2,1,0:T(8,128)S(1)}, f32[5,2,32,256]{3,2,1,0:T(8,128)S(1)}, u32[]{:S(2)}, u32[]{:S(2)}) %collective-permute-start.5) | collective-permute-done | bytes 327712 | tf_op jit(solution)/shard_map/ppermute | solution.py:21
  75.1 0.1 collective-permute-start.7
  75.1 0.5 collective-permute-start.6
  75.6 0.1 pad_maximum_fusion.1
  75.7 0.1 add_dynamic-update-slice_fusion
  76.0 0.2 maximum_maximum_fusion
  76.3 0.1 collective-permute-done.7
  76.4 0.2 collective-permute-done.6
  76.6 0.1 multiply_dynamic-update-slice_fusion.8
  76.7 0.1 add_dynamic-update-slice_fusion.2
  76.8 0.1 multiply_dynamic-update-slice_fusion.6
  76.9 0.8 %fusion.2 = f32[5,4,32,256]{3,2,1,0:T(8,128)S(1)} fusion(f32[5,4,36,256]{3,2,1,0:T(8,128)S(1)} %multiply_dynamic-update-slice_fusion.6, f32[5,8,32,256]{3,2,1,0:T(8,128)S(1)} %multiply_dynamic-update-slice_fusion, f32[5,4,32,254]{3,2,1,0:T(8,128)S(1)} %get-tuple-element.42, f32[5,4,32,2]{3,2,1,0:T(8,128)S(1)} %get-tuple-element.44, ...), kind=kLoop, calls=%fused_computation.23 | loop fusion | flops 3604480 | bytes 8519680 | tf_op jit(solution)/shard_map/add | solution.py:101
  77.8 0.8 %fusion.31 = f32[4,4,32,256]{3,2,1,0:T(8,128)S(1)} fusion(f32[5,8,2,256]{3,2,1,0:T(2,128)S(1)} %collective-permute-done.7, f32[5,2,32,256]{3,2,1,0:T(8,128)S(1)} %collective-permute-done.5, f32[5,2,32,256]{3,2,1,0:T(8,128)S(1)} %collective-permute-done.4, f32[1,4,32,256]{3,2,1,0:T(8,128)S(1)} %get-tuple-element.50, ...), kind=kLoop, calls=%fused_computation.74 | loop fusion | flops 6815744 | bytes 6717440 | tf_op jit(solution)/shard_map/add | solution.py:107
  78.6 0.2 fusion.21
  78.9 0.9 %pad_maximum_fusion.4 = f32[5,4,32,256]{3,2,1,0:T(8,128)} fusion(f32[1,4,32,256]{3,2,1,0:T(8,128)S(1)} %get-tuple-element.40, f32[3,4,32,256]{3,2,1,0:T(8,128)S(1)} %slice_divide_fusion, f32[1,4,32,256]{3,2,1,0:T(8,128)S(1)} %get-tuple-element.39), kind=kLoop, calls=%fused_computation.63 | loop fusion | flops 327680 | bytes 1310720 | tf_op jit(solution)/shard_map/concatenate | solution.py:111
  (49 shorter events, 1.1 us)
Async XLA Ops:
  0.0 8.0 %copy-start = (f32[5,4,32,256]{3,2,1,0:T(8,128)S(1)}, f32[5,4,32,256]{3,2,1,0:T(8,128)}, u32[]{:S(2)}) copy-start(f32[5,4,32,256]{3,2,1,0:T(8,128)} %param.3) | copy-start | bytes 1966084
  2.1 46.2 %collective-permute-start = (f32[5,2,32,256]{3,2,1,0:T(8,128)}, f32[5,2,32,256]{3,2,1,0:T(8,128)}, u32[]{:S(2)}, u32[]{:S(2)}) collective-permute-start(f32[5,2,32,256]{3,2,1,0:T(8,128)} %get-tuple-element.76), channel_id=1, source_target_pairs={{0,2},{2,4},{4,6},{6,8},{8,10},{10,12},{12,14},{14,0},{1,3},{3,5},... | collective-permute-start | bytes 983048 | tf_op jit(solution)/shard_map/ppermute | solution.py:18
  5.0 44.6 %collective-permute-start.1 = (f32[5,2,32,256]{3,2,1,0:T(8,128)}, f32[5,2,32,256]{3,2,1,0:T(8,128)}, u32[]{:S(2)}, u32[]{:S(2)}) collective-permute-start(f32[5,2,32,256]{3,2,1,0:T(8,128)} %get-tuple-element.75), channel_id=1, source_target_pairs={{2,0},{4,2},{6,4},{8,6},{10,8},{12,10},{14,12},{0,14},{3,1},{5,3},... | collective-permute-start | bytes 983048 | tf_op jit(solution)/shard_map/ppermute | solution.py:21
  13.7 33.6 %copy-start.12 = (f32[256]{0:T(256)S(1)}, f32[256]{0:T(256)}, u32[]{:S(2)}) copy-start(f32[256]{0:T(256)} %param.5) | copy-start | bytes 3076
  50.7 1.3 %collective-permute-start.3 = (f32[5,8,2,256]{3,2,1,0:T(2,128)S(1)}, f32[5,8,2,256]{3,2,1,0:T(2,128)S(1)}, u32[]{:S(2)}, u32[]{:S(2)}) collective-permute-start(f32[5,8,2,256]{3,2,1,0:T(2,128)S(1)} %get-tuple-element.38), channel_id=1, source_target_pairs={{1,0},{0,1},{3,2},{2,3},{5,4},{4,5},{7,6},{6,7},{9,8},{8,9},{11,10... | collective-permute-start | bytes 245768 | tf_op jit(solution)/shard_map/ppermute | solution.py:21
  50.8 1.4 %collective-permute-start.2 = (f32[5,8,2,256]{3,2,1,0:T(2,128)S(1)}, f32[5,8,2,256]{3,2,1,0:T(2,128)S(1)}, u32[]{:S(2)}, u32[]{:S(2)}) collective-permute-start(f32[5,8,2,256]{3,2,1,0:T(2,128)S(1)} %get-tuple-element.37), channel_id=1, source_target_pairs={{0,1},{1,0},{2,3},{3,2},{4,5},{5,4},{6,7},{7,6},{8,9},{9,8},{10,11... | collective-permute-start | bytes 245768 | tf_op jit(solution)/shard_map/ppermute | solution.py:18
  52.4 1.0 %copy-start.5 = (f32[5,4,32,2]{3,2,1,0:T(8,128)S(1)}, f32[5,4,32,2]{3,2,1,0:T(8,128)}, u32[]{:S(2)}) copy-start(f32[5,4,32,2]{3,2,1,0:T(8,128)} %get-tuple-element.66) | copy-start | bytes 15364
  52.4 1.1 %copy-start.6 = (f32[5,4,32,2]{3,2,1,0:T(8,128)S(1)}, f32[5,4,32,2]{3,2,1,0:T(8,128)}, u32[]{:S(2)}) copy-start(f32[5,4,32,2]{3,2,1,0:T(8,128)} %get-tuple-element.67) | copy-start | bytes 15364
  52.5 1.2 %copy-start.7 = (f32[5,4,32,1]{3,2,1,0:T(8,128)S(1)}, f32[5,4,32,1]{3,2,1,0:T(8,128)}, u32[]{:S(2)}) copy-start(f32[5,4,32,1]{3,2,1,0:T(8,128)} %get-tuple-element.70) | copy-start | bytes 7684
  52.5 1.2 %copy-start.8 = (f32[5,4,32,1]{3,2,1,0:T(8,128)S(1)}, f32[5,4,32,1]{3,2,1,0:T(8,128)}, u32[]{:S(2)}) copy-start(f32[5,4,32,1]{3,2,1,0:T(8,128)} %get-tuple-element.71) | copy-start | bytes 7684
  53.7 1.0 %copy-start.1 = (f32[4,4,32,254]{3,2,1,0:T(8,128)S(1)}, f32[4,4,32,254]{3,2,1,0:T(8,128)}, u32[]{:S(2)}) copy-start(f32[4,4,32,254]{3,2,1,0:T(8,128)} %get-tuple-element.56) | copy-start | bytes 1560580
  53.7 1.2 %copy-start.2 = (f32[4,4,32,254]{3,2,1,0:T(8,128)S(1)}, f32[4,4,32,254]{3,2,1,0:T(8,128)}, u32[]{:S(2)}) copy-start(f32[4,4,32,254]{3,2,1,0:T(8,128)} %get-tuple-element.57) | copy-start | bytes 1560580
  53.7 1.4 %copy-start.3 = (f32[4,4,32,255]{3,2,1,0:T(8,128)S(1)}, f32[4,4,32,255]{3,2,1,0:T(8,128)}, u32[]{:S(2)}) copy-start(f32[4,4,32,255]{3,2,1,0:T(8,128)} %get-tuple-element.60) | copy-start | bytes 1566724
  53.7 1.5 %copy-start.4 = (f32[4,4,32,255]{3,2,1,0:T(8,128)S(1)}, f32[4,4,32,255]{3,2,1,0:T(8,128)}, u32[]{:S(2)}) copy-start(f32[4,4,32,255]{3,2,1,0:T(8,128)} %get-tuple-element.61) | copy-start | bytes 1566724
  53.7 1.6 %copy-start.9 = (f32[4,4,32,2]{3,2,1,0:T(8,128)S(1)}, f32[4,4,32,2]{3,2,1,0:T(8,128)}, u32[]{:S(2)}) copy-start(f32[4,4,32,2]{3,2,1,0:T(8,128)} %get-tuple-element.59) | copy-start | bytes 12292
  53.7 1.6 %copy-start.10 = (f32[4,4,32,1]{3,2,1,0:T(8,128)S(1)}, f32[4,4,32,1]{3,2,1,0:T(8,128)}, u32[]{:S(2)}) copy-start(f32[4,4,32,1]{3,2,1,0:T(8,128)} %get-tuple-element.62) | copy-start | bytes 6148
  53.7 1.7 %copy-start.11 = (f32[4,4,32,1]{3,2,1,0:T(8,128)S(1)}, f32[4,4,32,1]{3,2,1,0:T(8,128)}, u32[]{:S(2)}) copy-start(f32[4,4,32,1]{3,2,1,0:T(8,128)} %get-tuple-element.63) | copy-start | bytes 6148
  57.9 17.0 %collective-permute-start.5 = (f32[5,2,32,256]{3,2,1,0:T(8,128)S(1)}, f32[5,2,32,256]{3,2,1,0:T(8,128)S(1)}, u32[]{:S(2)}, u32[]{:S(2)}) collective-permute-start(f32[5,2,32,256]{3,2,1,0:T(8,128)S(1)} %get-tuple-element.55), channel_id=1, source_target_pairs={{2,0},{4,2},{6,4},{8,6},{10,8},{12,10},{14,12},{0,14},{3,1},{5,3},... | collective-permute-start | bytes 983048 | tf_op jit(solution)/shard_map/ppermute | solution.py:21
  58.0 17.0 %collective-permute-start.4 = (f32[5,2,32,256]{3,2,1,0:T(8,128)S(1)}, f32[5,2,32,256]{3,2,1,0:T(8,128)S(1)}, u32[]{:S(2)}, u32[]{:S(2)}) collective-permute-start(f32[5,2,32,256]{3,2,1,0:T(8,128)S(1)} %get-tuple-element.54), channel_id=1, source_target_pairs={{0,2},{2,4},{4,6},{6,8},{8,10},{10,12},{12,14},{14,0},{1,3},{3,5},... | collective-permute-start | bytes 983048 | tf_op jit(solution)/shard_map/ppermute | solution.py:18
  75.1 1.3 %collective-permute-start.7 = (f32[5,8,2,256]{3,2,1,0:T(2,128)S(1)}, f32[5,8,2,256]{3,2,1,0:T(2,128)S(1)}, u32[]{:S(2)}, u32[]{:S(2)}) collective-permute-start(f32[5,8,2,256]{3,2,1,0:T(2,128)S(1)} %get-tuple-element.36), channel_id=1, source_target_pairs={{1,0},{0,1},{3,2},{2,3},{5,4},{4,5},{7,6},{6,7},{9,8},{8,9},{11,10... | collective-permute-start | bytes 245768 | tf_op jit(solution)/shard_map/ppermute | solution.py:21
  75.1 1.4 %collective-permute-start.6 = (f32[5,8,2,256]{3,2,1,0:T(2,128)S(1)}, f32[5,8,2,256]{3,2,1,0:T(2,128)S(1)}, u32[]{:S(2)}, u32[]{:S(2)}) collective-permute-start(f32[5,8,2,256]{3,2,1,0:T(2,128)S(1)} %get-tuple-element.35), channel_id=1, source_target_pairs={{0,1},{1,0},{2,3},{3,2},{4,5},{5,4},{6,7},{7,6},{8,9},{9,8},{10,11... | collective-permute-start | bytes 245768 | tf_op jit(solution)/shard_map/ppermute | solution.py:18
where the time goes:
time: 80.1 us; the launch traced here: 79.8 us
  blocking collectives  31.2 us (39%)
  waiting for transfers between devices  15.5 us (19%)
  local copies, waits for them, and re-layouts  13.7 us (17%)
  starting transfers between devices  9.19 us (11%)
  other arithmetic  9.04 us (11%)
  between operations  1.18 us (1%)
    pmax x1, blocking collectives, per_device(): fastest = lax.pmax(jnp.max(speeds(conserved)), ('gx', 'gy'))  31.2 us
    ppermute x4, waiting for transfers between devices, extended(): lax.ppermute(lax.slice_in_dim(block, 0, width, axis=dim), axis, backward)  15.2 us
    ppermute x4, starting transfers between devices, extended(): lax.ppermute(lax.slice_in_dim(block, block.shape[dim] - width, None, axis...  5.94 us
    ppermute x4, starting transfers between devices, extended(): lax.ppermute(lax.slice_in_dim(block, 0, width, axis=dim), axis, backward)  3.24 us
    unnamed x31, local copies, waits for them, and re-layouts  3.08 us
    slice x1, local copies, waits for them, and re-layouts, extended(): lax.slice_in_dim(block, 0, width, axis=dim)  2.05 us
    slice x2, local copies, waits for them, and re-layouts, roll_curve(): jnp.roll(values, -1, 3)  2.04 us
    slice x2, local copies, waits for them, and re-layouts, roll_curve(): jnp.roll(values, -2, 3)  1.98 us
  transfers between devices with their start and end apart: 8, of which 5 were waited for; matrix products, arithmetic and copies ran while one was open for 14% of the time, Pallas kernels for 0%

commit v1 on v0

v1 whole, which is shorter than its diff:
```python
import functools

import jax
import jax.numpy as jnp
from jax import lax
from jax.experimental import pallas as pl
from jax.experimental.pallas import tpu as pltpu
from jax.sharding import PartitionSpec as P

GAMMA_LESS = 0.4
GAMMA_FULL = 1.4
COURANT = 0.3
VISCOSITY = 0.05
MESH = pl.DeviceIdType.MESH
EDGE = 8


def rolled(value, shift, axis):
    return pltpu.roll(value, shift % value.shape[axis], axis)


def primitives(read):
    rho, m0, m1, m2, energy = [read(c) for c in range(5)]
    inverse = 1.0 / rho
    squares = m0 * m0 + m1 * m1 + m2 * m2
    pressure = GAMMA_LESS * (energy - 0.5 * squares * inverse)
    return rho, (m0, m1, m2), energy, inverse, squares, pressure


def flux(momenta, energy, inverse, pressure, k):
    w = momenta[k] * inverse
    parts = [momenta[k]] + [m * w for m in momenta] + [(energy + pressure) * w]
    parts[1 + k] = parts[1 + k] + pressure
    return parts


def rolled_terms(f, q, axis):
    if q is None:
        return (
            8.0 * (rolled(f, 1, axis) - rolled(f, -1, axis))
            - (rolled(f, 2, axis) - rolled(f, -2, axis))
        )
    s = VISCOSITY * q
    big, wide = 8.0 * f, 16.0 * s
    return (
        rolled(wide + big, 1, axis)
        + rolled(wide - big, -1, axis)
        - rolled(s + f, 2, axis)
        - rolled(s - f, -2, axis)
    )


def kernel(n, q_hbm, mask_hbm, penalty, out, state, mask, fluxes, stage, best,
           local_sem, sx, rx, sz, rz, sy, ry, sm, rm):
    i = lax.axis_index("gx")
    g = lax.axis_index("gy")
    layers, rows, width = q_hbm.shape[1:]
    lo, hi, tall = EDGE, EDGE + rows, rows + 2 * EDGE
    half = layers // 2
    parity = lax.rem(i, 2)
    partner = i + 1 - 2 * parity
    sibling = 1 - g
    z_to = lax.rem(i + 2 - 4 * parity + n, n)
    z_from = lax.rem(i - 2 + 4 * parity + n, n)
    steps = n.bit_length() - 1
    flips = [i + (1 << k) * (1 - 2 * lax.rem(i // (1 << k), 2)) for k in range(steps)]

    local_q = pltpu.make_async_copy(
        q_hbm, state.at[:, layers:2 * layers, lo:hi, :], local_sem.at[0])
    local_m = pltpu.make_async_copy(
        mask_hbm, mask.at[layers:2 * layers, lo:hi, :], local_sem.at[1])
    local_q.start()
    local_m.start()

    barrier = pltpu.get_barrier_semaphore()
    others = [partner, z_to, z_from] + flips[1:]
    for j in others:
        pl.semaphore_signal(barrier, inc=1, device_id={"gx": j}, device_id_type=MESH)
    pl.semaphore_signal(barrier, inc=1, device_id={"gy": sibling}, device_id_type=MESH)
    pl.semaphore_wait(barrier, len(others) + 1)

    def remote(src, dst, send, recv, where):
        return pltpu.make_async_remote_copy(
            src_ref=src, dst_ref=dst, send_sem=send, recv_sem=recv,
            device_id=where, device_id_type=MESH)

    own = (half * parity, half - half * parity)
    seen = (half - half * parity, half * parity)
    x_out, x_in = 2 * layers * parity, 2 * layers * (1 - parity)
    z_out = z_in = 2 * layers * parity
    pieces = [(h, c) for h in range(2) for c in range(-1, 5)]
    x_sends, x_waits, z_sends, z_waits = [], [], [], []
    for k, (h, c) in enumerate(pieces):
        def x_copy(start, where):
            if c < 0:
                return remote(
                    mask_hbm.at[pl.ds(start, half)],
                    mask.at[pl.ds(where + start, half), lo:hi, :],
                    sx.at[k], rx.at[k], {"gx": partner})
            return remote(
                q_hbm.at[c, pl.ds(start, half)],
                state.at[c, pl.ds(where + start, half), lo:hi, :],
                sx.at[k], rx.at[k], {"gx": partner})

        def z_copy(start, source, target):
            if c < 0:
                return remote(
                    mask.at[pl.ds(source + start, half), lo:hi, :],
                    mask.at[pl.ds(target + start, half), lo:hi, :],
                    sz.at[k], rz.at[k], {"gx": z_to})
            return remote(
                state.at[c, pl.ds(source + start, half), lo:hi, :],
                state.at[c, pl.ds(target + start, half), lo:hi, :],
                sz.at[k], rz.at[k], {"gx": z_to})

        x_sends.append(x_copy(own[h], x_out))
        x_waits.append(x_copy(seen[h], x_in))
        if c < 0 and h == 1:
            z_sends.append(None)
            z_waits.append(None)
        else:
            z_sends.append(z_copy(seen[h], x_in, z_out))
            z_waits.append(z_copy(seen[h], z_in, z_in))

    for copy in x_sends:
        copy.start()

    to_sibling = {"gy": sibling}
    edges = [
        remote(q_hbm.at[:, :, 0:EDGE, :], state.at[:, layers:2 * layers, hi:tall, :],
               sy.at[0], ry.at[0], to_sibling),
        remote(q_hbm.at[:, :, rows - EDGE:rows, :], state.at[:, layers:2 * layers, 0:lo, :],
               sy.at[1], ry.at[1], to_sibling),
        remote(mask_hbm.at[:, 0:EDGE, :], mask.at[layers:2 * layers, hi:tall, :],
               sy.at[2], ry.at[2], to_sibling),
        remote(mask_hbm.at[:, rows - EDGE:rows, :], mask.at[layers:2 * layers, 0:lo, :],
               sy.at[3], ry.at[3], to_sibling),
    ]

    def corner(where, k):
        spot = pl.ds(where, half)
        return [
            remote(state.at[:, spot, lo:lo + EDGE, :], state.at[:, spot, hi:tall, :],
                   sy.at[k], ry.at[k], to_sibling),
            remote(state.at[:, spot, hi - EDGE:hi, :], state.at[:, spot, 0:lo, :],
                   sy.at[k + 1], ry.at[k + 1], to_sibling),
        ]

    corner_z = corner(z_in + seen[0], 4)
    corner_x = corner(x_in + seen[1], 6)
    for copy in edges:
        copy.start()
    local_q.wait()

    def speed_step(l, top):
        rho, _, _, inverse, squares, pressure = primitives(
            lambda c: state[c, layers + l, lo:hi, :])
        speed = jnp.sqrt(squares * inverse * inverse) + jnp.sqrt(
            GAMMA_FULL * pressure * inverse)
        for r in range(0, rows, 8):
            for z in range(0, width, 128):
                top = jnp.maximum(top, speed[r:r + 8, z:z + 128])
        return top

    best[0] = lax.fori_loop(0, layers, speed_step, jnp.zeros((8, 128), jnp.float32))

    def max_copy(k):
        where = {"gy": sibling} if k == 0 else {"gx": flips[k - 1]}
        return remote(best.at[2 * k], best.at[2 * k + 1], sm.at[k], rm.at[k], where)

    def max_finish(k):
        max_copies[k].wait_recv()
        best[2 * k + 2] = jnp.maximum(best[2 * k], best[2 * k + 1])

    max_copies = [max_copy(k) for k in range(steps + 1)]
    max_copies[0].start()
    done = 0
    for k, (h, c) in enumerate(pieces):
        x_waits[k].wait_recv()
        if z_sends[k] is not None:
            z_sends[k].start()
        if done <= steps and k >= 1:
            max_finish(done)
            done += 1
            if done <= steps:
                max_copies[done].start()
    for copy in corner_x:
        copy.start()
    for k in range(6):
        z_waits[k].wait_recv()
    for copy in corner_z:
        copy.start()
    while done <= steps:
        max_finish(done)
        done += 1
        if done <= steps:
            max_copies[done].start()
    for k in range(6, 12):
        if z_waits[k] is not None:
            z_waits[k].wait_recv()
    local_m.wait()
    for copy in edges + corner_x + corner_z:
        copy.wait_recv()

    top = jnp.max(best[2 * steps + 2], axis=1, keepdims=True)
    time_step = COURANT / jnp.max(top, axis=0, keepdims=True)
    scale = time_step / 12.0
    rates = penalty[...]

    def store_flux(source, first, last):
        def store(l, carry):
            _, momenta, energy, inverse, _, pressure = primitives(
                lambda c: source[c, l, first:last, :])
            parts = flux(momenta, energy, inverse, pressure, 0)
            for c in range(1, 5):
                fluxes[c - 1, l, first:last, :] = parts[c]
            return carry
        return store

    def change(source, l, first, last):
        _, momenta, energy, inverse, _, pressure = primitives(lambda c: source[c, l])
        fy = flux(momenta, energy, inverse, pressure, 1)
        inner = slice(first, last)
        fz = flux([m[inner] for m in momenta], energy[inner], inverse[inner], pressure[inner], 2)
        results = []
        for c in range(5):
            q = None if c == 0 else source[c, l]
            total = rolled_terms(fy[c], q, 0)[inner]
            if c == 0:
                total = total + rolled_terms(fz[c], None, 1)
                near = lambda d: source[1, l + d, first:last, :]
            else:
                total = total + rolled_terms(fz[c], q[inner], 1)
                near = lambda d: fluxes[c - 1, l + d, first:last, :]
            total = total + 8.0 * (near(-1) - near(1)) - (near(-2) - near(2))
            if c > 0:
                beside = lambda d: source[c, l + d, first:last, :]
                total = total + VISCOSITY * (
                    16.0 * (beside(-1) + beside(1)) - (beside(-2) + beside(2)) - 90.0 * q[inner])
            results.append(total)
        return results

    def damping(l, first, last):
        brinkman = mask[l, first:last, :].astype(jnp.float32) * rates
        return 1.0 / (1.0 + time_step * brinkman)

    def section_one(first, last):
        def body(l, carry):
            damp = damping(l, first, last)
            for c, total in enumerate(change(state, l, first, last)):
                value = state[c, l, first:last, :] + scale * total
                stage[c, l, first:last, :] = value * damp if 1 <= c <= 3 else value
            return carry
        return body

    near, far = layers - half, 2 * layers + half
    lax.fori_loop(0, near, store_flux(state, lo, hi), 0)
    lax.fori_loop(near, far, store_flux(state, 0, tall), 0)
    lax.fori_loop(far, 3 * layers, store_flux(state, lo, hi), 0)
    lax.fori_loop(near, layers, section_one(lo, hi), 0)
    lax.fori_loop(layers, 2 * layers, section_one(0, tall), 0)
    lax.fori_loop(2 * layers, far, section_one(lo, hi), 0)

    lax.fori_loop(near, far, store_flux(stage, lo, hi), 0)

    def section_two(t, carry):
        l = layers + t
        damp = damping(l, lo, hi)
        for c, total in enumerate(change(stage, l, lo, hi)):
            value = 0.5 * state[c, l, lo:hi, :] + 0.5 * (
                stage[c, l, lo:hi, :] + scale * total)
            out[c, t] = value * damp if 1 <= c <= 3 else value
        return carry

    lax.fori_loop(0, layers, section_two, 0)

    for copy in x_sends + edges + corner_x + corner_z + max_copies:
        copy.wait_send()
    for copy in z_sends:
        if copy is not None:
            copy.wait_send()


def per_device(n, conserved, solid_mask, penalty):
    _, layers, rows, width = conserved.shape
    tall = rows + 2 * EDGE
    steps = n.bit_length() - 1
    dma = pltpu.SemaphoreType.DMA
    return pl.pallas_call(
        functools.partial(kernel, n),
        out_shape=jax.ShapeDtypeStruct(conserved.shape, jnp.float32),
        in_specs=[
            pl.BlockSpec(memory_space=pl.ANY),
            pl.BlockSpec(memory_space=pl.ANY),
            pl.BlockSpec(memory_space=pltpu.VMEM),
        ],
        out_specs=pl.BlockSpec(memory_space=pltpu.VMEM),
        scratch_shapes=[
            pltpu.VMEM((5, 3 * layers, tall, width), jnp.float32),
            pltpu.VMEM((3 * layers, tall, width), jnp.int32),
            pltpu.VMEM((4, 3 * layers, tall, width), jnp.float32),
            pltpu.VMEM((5, 3 * layers, tall, width), jnp.float32),
            pltpu.VMEM((2 * steps + 3, 8, 128), jnp.float32),
            dma((2,)),
            dma((12,)), dma((12,)),
            dma((12,)), dma((12,)),
            dma((8,)), dma((8,)),
            dma((steps + 1,)), dma((steps + 1,)),
        ],
        compiler_params=pltpu.CompilerParams(
            collective_id=0, has_side_effects=True, vmem_limit_bytes=40 * 1024 * 1024),
    )(conserved, solid_mask, penalty.reshape(1, width))


def solution(mesh):
    return jax.shard_map(
        functools.partial(per_device, mesh.shape["gx"]),
        mesh=mesh,
        in_specs=(
            P(None, ("member", "gx"), "gy", None),
            P(("member", "gx"), "gy", None),
            P("member"),
        ),
        out_specs=P(None, ("member", "gx"), "gy", None),
        check_vma=False,
    )
```

time: 80.1 us -> 48.2 us (0.60)
  Pallas kernels: 0 us -> 44.5 us
  blocking collectives: 31.2 us -> 0 us
  waiting for transfers between devices: 15.5 us -> 0 us
  local copies, waits for them, and re-layouts: 13.7 us -> 3.51 us
  starting transfers between devices: 9.19 us -> 0 us
  other arithmetic: 9.04 us -> 0 us
  between operations: 1.18 us -> 0.01 us
    pallas_call x0 -> x1, Pallas kernels: none -> 44.5 us  [per_device(): pl.pallas_call(functools.partial(kernel, n), out_shape=jax.ShapeDtypeStru...]
    pmax x1 -> x0, blocking collectives: 31.2 us -> none  [per_device(): fastest = lax.pmax(jnp.max(speeds(conserved)), ('gx', 'gy'))]
    ppermute x8 -> x0, waiting for transfers between devices: 15.5 us -> none  [the longest x4 15.2 us: extended(): lax.ppermute(lax.slice_in_dim(block, 0, width, axis=dim), axis, backward)]
    slice x16 -> x0, local copies, waits for them, and re-layouts: 9.37 us -> none  [the longest x1 2.05 us: extended(): lax.slice_in_dim(block, 0, width, axis=dim)]
    ppermute x8 -> x0, starting transfers between devices: 9.19 us -> none  [the longest x4 5.94 us: extended(): lax.ppermute(lax.slice_in_dim(block, block.shape[dim] - width, None, axis...]
    add x7 -> x0, other arithmetic: 4.57 us -> none  [the longest x2 1.69 us: operate(): -divergence[1:] + VISCOSITY * diffusion]
    concatenate x8 -> x0, other arithmetic: 1.96 us -> none  [the longest x6 1.64 us: damp_momenta(): jnp.concatenate([fields[:1], fields[1:4] / (1.0 + time_step * brinkman),...]
    concatenate x2 -> x0, local copies, waits for them, and re-layouts: 1.26 us -> none  [extended(): block = jnp.concatenate([low, block, high], axis=dim)]
  transfers between devices with their start and end apart: 8 -> 0, of which waited for: 5 -> 0; matrix products, arithmetic and copies ran while one was open for 14% -> 0% of each run, Pallas kernels for 0% -> 0%
where the time goes in v1:
time: 48.2 us; the launch traced here: 48 us
  Pallas kernels  44.5 us (92%)
  local copies, waits for them, and re-layouts  3.51 us (7%)
    pallas_call x1, Pallas kernels, per_device(): pl.pallas_call(functools.partial(kernel, n), out_shape=jax.ShapeDtypeStru...  44.5 us
    unnamed x7, local copies, waits for them, and re-layouts  3.51 us

profile of v1, /device:TPU:0, one launch (start us, length us, event | category | flops | bytes accessed | tf_op | source)
XLA Modules:
  0.0 48.0 jit_solution(12762300600891993201)
XLA Ops:
  0.0 0.0 copy-start.2
  0.0 0.7 %copy-done.2 = f32[256]{0:T(256)S(1)} copy-done((f32[256]{0:T(256)S(1)}, f32[256]{0:T(256)}, u32[]{:S(2)}) %copy-start.2) | copy-done | bytes 1048
  0.7 0.0 copy-start
  0.7 1.1 %copy-done = f32[5,4,32,256]{3,2,1,0:T(8,128)S(1)} copy-done((f32[5,4,32,256]{3,2,1,0:T(8,128)S(1)}, f32[5,4,32,256]{3,2,1,0:T(8,128)}, u32[]{:S(2)}) %copy-start) | copy-done | bytes 655384
  1.8 0.0 copy-start.1
  1.8 0.9 %copy-done.1 = s32[4,32,256]{2,1,0:T(8,128)S(1)} copy-done((s32[4,32,256]{2,1,0:T(8,128)S(1)}, s32[4,32,256]{2,1,0:T(8,128)}, u32[]{:S(2)}) %copy-start.1) | copy-done | bytes 131096
  2.7 44.5 %shard_map.37 = f32[5,4,32,256]{3,2,1,0:T(8,128)S(1)} custom-call(f32[5,4,32,256]{3,2,1,0:T(8,128)S(1)} %copy-done, s32[4,32,256]{2,1,0:T(8,128)S(1)} %copy-done.1, f32[1,256]{1,0:T(1,128)S(1)} %bitcast.1), custom_call_target="tpu_custom_call" | custom-call | tf_op jit(solution)/shard_map/pallas_call | solution.py:289
  47.2 0.8 %copy.5 = f32[5,4,32,256]{3,2,1,0:T(8,128)} copy(f32[5,4,32,256]{3,2,1,0:T(8,128)S(1)} %shard_map.37) | data formatting | bytes 1310720
Async XLA Ops:
  0.0 0.7 %copy-start.2 = (f32[256]{0:T(256)S(1)}, f32[256]{0:T(256)}, u32[]{:S(2)}) copy-start(f32[256]{0:T(256)} %param.5) | copy-start | bytes 3076
  0.7 1.1 %copy-start = (f32[5,4,32,256]{3,2,1,0:T(8,128)S(1)}, f32[5,4,32,256]{3,2,1,0:T(8,128)}, u32[]{:S(2)}) copy-start(f32[5,4,32,256]{3,2,1,0:T(8,128)} %q_hbm.1) | copy-start | bytes 1966084
  1.8 0.9 %copy-start.1 = (s32[4,32,256]{2,1,0:T(8,128)S(1)}, s32[4,32,256]{2,1,0:T(8,128)}, u32[]{:S(2)}) copy-start(s32[4,32,256]{2,1,0:T(8,128)} %mask_hbm.1) | copy-start | bytes 393220

commit v2 on v1

--- a/solution.py
+++ b/solution.py
@@ -13,6 +13,7 @@
 VISCOSITY = 0.05
 MESH = pl.DeviceIdType.MESH
 EDGE = 8
+AHEAD = 4
 
 
 def rolled(value, shift, axis):
@@ -50,7 +51,7 @@
     )
 
 
-def kernel(n, q_hbm, mask_hbm, penalty, out, state, mask, fluxes, stage, best,
+def kernel(n, q_hbm, mask_hbm, penalty, out, state, mask, fluxes, fluxes_two, stage, part, best,
            local_sem, sx, rx, sz, rz, sy, ry, sm, rm):
     i = lax.axis_index("gx")
     g = lax.axis_index("gy")
@@ -62,8 +63,7 @@
     sibling = 1 - g
     z_to = lax.rem(i + 2 - 4 * parity + n, n)
     z_from = lax.rem(i - 2 + 4 * parity + n, n)
-    steps = n.bit_length() - 1
-    flips = [i + (1 << k) * (1 - 2 * lax.rem(i // (1 << k), 2)) for k in range(steps)]
+    level = [lax.rem(i + 2 * m, n) for m in range(1, n // 2)]
 
     local_q = pltpu.make_async_copy(
         q_hbm, state.at[:, layers:2 * layers, lo:hi, :], local_sem.at[0])
@@ -73,11 +73,11 @@
     local_m.start()
 
     barrier = pltpu.get_barrier_semaphore()
-    others = [partner, z_to, z_from] + flips[1:]
-    for j in others:
-        pl.semaphore_signal(barrier, inc=1, device_id={"gx": j}, device_id_type=MESH)
-    pl.semaphore_signal(barrier, inc=1, device_id={"gy": sibling}, device_id_type=MESH)
-    pl.semaphore_wait(barrier, len(others) + 1)
+    near_by = [{"gy": sibling}, {"gx": partner}, {"gx": partner, "gy": sibling}]
+    others = near_by + [{"gx": j} for j in level]
+    for where in others:
+        pl.semaphore_signal(barrier, inc=1, device_id=where, device_id_type=MESH)
+    pl.semaphore_wait(barrier, len(others))
 
     def remote(src, dst, send, recv, where):
         return pltpu.make_async_remote_copy(
@@ -122,7 +122,7 @@
             z_sends.append(z_copy(seen[h], x_in, z_out))
             z_waits.append(z_copy(seen[h], z_in, z_in))
 
-    for copy in x_sends:
+    for copy in x_sends[:AHEAD]:
         copy.start()
 
     to_sibling = {"gy": sibling}
@@ -165,114 +165,155 @@
     best[0] = lax.fori_loop(0, layers, speed_step, jnp.zeros((8, 128), jnp.float32))
 
     def max_copy(k):
-        where = {"gy": sibling} if k == 0 else {"gx": flips[k - 1]}
-        return remote(best.at[2 * k], best.at[2 * k + 1], sm.at[k], rm.at[k], where)
-
-    def max_finish(k):
-        max_copies[k].wait_recv()
-        best[2 * k + 2] = jnp.maximum(best[2 * k], best[2 * k + 1])
-
-    max_copies = [max_copy(k) for k in range(steps + 1)]
-    max_copies[0].start()
-    done = 0
-    for k, (h, c) in enumerate(pieces):
-        x_waits[k].wait_recv()
-        if z_sends[k] is not None:
-            z_sends[k].start()
-        if done <= steps and k >= 1:
-            max_finish(done)
-            done += 1
-            if done <= steps:
-                max_copies[done].start()
-    for copy in corner_x:
+        source = 0 if k < 3 else 4
+        return remote(best.at[source], best.at[k + 1 if k < 3 else k + 2],
+                      sm.at[k], rm.at[k], others[k])
+
+    max_copies = [max_copy(k) for k in range(len(others))]
+    for copy in max_copies[:3]:
         copy.start()
-    for k in range(6):
-        z_waits[k].wait_recv()
-    for copy in corner_z:
-        copy.start()
-    while done <= steps:
-        max_finish(done)
-        done += 1
-        if done <= steps:
-            max_copies[done].start()
-    for k in range(6, 12):
-        if z_waits[k] is not None:
-            z_waits[k].wait_recv()
-    local_m.wait()
-    for copy in edges + corner_x + corner_z:
-        copy.wait_recv()
-
-    top = jnp.max(best[2 * steps + 2], axis=1, keepdims=True)
-    time_step = COURANT / jnp.max(top, axis=0, keepdims=True)
-    scale = time_step / 12.0
-    rates = penalty[...]
+
+    z_inner, z_outer = z_in + seen[0], z_in + seen[1]
+    x_outer, x_inner = x_in + seen[0], x_in + seen[1]
+    own_z = layers + half * parity
+    own_x = layers + half * (1 - parity)
+
+    def each(start, count, body):
+        def step(t, carry):
+            body(start + t)
+            return carry
+        lax.fori_loop(0, count, step, 0)
 
     def store_flux(source, first, last):
-        def store(l, carry):
+        target = fluxes if source is state else fluxes_two
+
+        def store(l):
             _, momenta, energy, inverse, _, pressure = primitives(
                 lambda c: source[c, l, first:last, :])
             parts = flux(momenta, energy, inverse, pressure, 0)
             for c in range(1, 5):
-                fluxes[c - 1, l, first:last, :] = parts[c]
-            return carry
+                target[c - 1, l, first:last, :] = parts[c]
         return store
 
-    def change(source, l, first, last):
-        _, momenta, energy, inverse, _, pressure = primitives(lambda c: source[c, l])
-        fy = flux(momenta, energy, inverse, pressure, 1)
+    def store_part(source, first, last):
         inner = slice(first, last)
-        fz = flux([m[inner] for m in momenta], energy[inner], inverse[inner], pressure[inner], 2)
-        results = []
+
+        def store(l):
+            _, momenta, energy, inverse, _, pressure = primitives(lambda c: source[c, l])
+            fy = flux(momenta, energy, inverse, pressure, 1)
+            fz = flux(
+                [m[inner] for m in momenta], energy[inner], inverse[inner], pressure[inner], 2)
+            for c in range(5):
+                q = None if c == 0 else source[c, l]
+                total = rolled_terms(fy[c], q, 0)[inner]
+                if c == 0:
+                    total = total + rolled_terms(fz[c], None, 1)
+                else:
+                    total = total + rolled_terms(fz[c], q[inner], 1)
+                    total = total - (90.0 * VISCOSITY) * q[inner]
+                part[c, l, first:last, :] = total
+        return store
+
+    def whole(source, c, l, first, last):
+        at = lambda ref, index, d: ref[index, l + d, first:last, :]
+        x_flux = fluxes if source is state else fluxes_two
+        f = (lambda d: at(source, 1, d)) if c == 0 else (lambda d: at(x_flux, c - 1, d))
+        total = part[c, l, first:last, :] + 8.0 * (f(-1) - f(1)) - (f(-2) - f(2))
+        if c > 0:
+            q = lambda d: at(source, c, d)
+            total = total + VISCOSITY * (16.0 * (q(-1) + q(1)) - (q(-2) + q(2)))
+        return total
+
+    def damping(l, first, last, time_step):
+        brinkman = mask[l, first:last, :].astype(jnp.float32) * penalty[...]
+        return 1.0 / (1.0 + time_step * brinkman)
+
+    def section_one(first, last, time_step):
+        scale = time_step / 12.0
+
+        def body(l):
+            damp = damping(l, first, last, time_step)
+            for c in range(5):
+                value = state[c, l, first:last, :] + scale * whole(state, c, l, first, last)
+                stage[c, l, first:last, :] = value * damp if 1 <= c <= 3 else value
+        return body
+
+    for k in range(len(pieces)):
+        x_waits[k].wait_recv()
+        if z_sends[k] is not None:
+            z_sends[k].start()
+        if k + AHEAD < len(pieces):
+            x_sends[k + AHEAD].start()
+        if k == 1:
+            for copy in max_copies[:3]:
+                copy.wait_recv()
+            best[4] = jnp.maximum(
+                jnp.maximum(best[0], best[1]), jnp.maximum(best[2], best[3]))
+            for copy in max_copies[3:]:
+                copy.start()
+            for copy in edges:
+                copy.wait_recv()
+            each(own_z, half, store_part(state, 0, tall))
+        if k == 2:
+            each(own_x, half, store_part(state, 0, tall))
+        if k == 3:
+            each(layers, layers, store_flux(state, 0, tall))
+        if k == 5:
+            each(x_outer, half, store_flux(state, lo, hi))
+        if k == 7:
+            for h in range(6):
+                z_waits[h].wait_recv()
+            for copy in corner_z:
+                copy.start()
+            for copy in max_copies[3:]:
+                copy.wait_recv()
+        if k == 8:
+            for copy in corner_z:
+                copy.wait_recv()
+            each(z_inner, half, store_flux(state, 0, tall))
+            each(z_inner, half, store_part(state, lo, hi))
+        if k == 9:
+            local_m.wait()
+            top = best[4]
+            for m in range(len(level)):
+                top = jnp.maximum(top, best[5 + m])
+            top = jnp.max(jnp.max(top, axis=1, keepdims=True), axis=0, keepdims=True)
+            time_step = COURANT / top
+            each(own_z, half, section_one(0, tall, time_step))
+        if k == 10:
+            each(own_z, half, store_part(stage, lo, hi))
+            each(own_z, half, store_flux(stage, lo, hi))
+
+    for copy in corner_x:
+        copy.start()
+    each(x_inner, half, store_flux(state, lo, hi))
+    each(own_x, half, section_one(lo, hi, time_step))
+    for k in range(7, 12):
+        z_waits[k].wait_recv()
+    each(z_outer, half, store_flux(state, lo, hi))
+    each(z_inner, half, section_one(lo, hi, time_step))
+    each(z_inner, half, store_flux(stage, lo, hi))
+    for copy in corner_x:
+        copy.wait_recv()
+    for first, last in ((0, lo), (hi, tall)):
+        each(x_inner, half, store_flux(state, first, last))
+        each(own_x, half, section_one(first, last, time_step))
+    each(x_inner, half, store_part(state, lo, hi))
+    each(x_inner, half, section_one(lo, hi, time_step))
+    each(x_inner, half, store_flux(stage, lo, hi))
+    each(own_x, half, store_part(stage, lo, hi))
+    each(own_x, half, store_flux(stage, lo, hi))
+
+    scale = time_step / 12.0
+
+    def section_two(l):
+        damp = damping(l, lo, hi, time_step)
         for c in range(5):
-            q = None if c == 0 else source[c, l]
-            total = rolled_terms(fy[c], q, 0)[inner]
-            if c == 0:
-                total = total + rolled_terms(fz[c], None, 1)
-                near = lambda d: source[1, l + d, first:last, :]
-            else:
-                total = total + rolled_terms(fz[c], q[inner], 1)
-                near = lambda d: fluxes[c - 1, l + d, first:last, :]
-            total = total + 8.0 * (near(-1) - near(1)) - (near(-2) - near(2))
-            if c > 0:
-                beside = lambda d: source[c, l + d, first:last, :]
-                total = total + VISCOSITY * (
-                    16.0 * (beside(-1) + beside(1)) - (beside(-2) + beside(2)) - 90.0 * q[inner])
-            results.append(total)
-        return results
-
-    def damping(l, first, last):
-        brinkman = mask[l, first:last, :].astype(jnp.float32) * rates
-        return 1.0 / (1.0 + time_step * brinkman)
-
-    def section_one(first, last):
-        def body(l, carry):
-            damp = damping(l, first, last)
-            for c, total in enumerate(change(state, l, first, last)):
-                value = state[c, l, first:last, :] + scale * total
-                stage[c, l, first:last, :] = value * damp if 1 <= c <= 3 else value
-            return carry
-        return body
-
-    near, far = layers - half, 2 * layers + half
-    lax.fori_loop(0, near, store_flux(state, lo, hi), 0)
-    lax.fori_loop(near, far, store_flux(state, 0, tall), 0)
-    lax.fori_loop(far, 3 * layers, store_flux(state, lo, hi), 0)
-    lax.fori_loop(near, layers, section_one(lo, hi), 0)
-    lax.fori_loop(layers, 2 * layers, section_one(0, tall), 0)
-    lax.fori_loop(2 * layers, far, section_one(lo, hi), 0)
-
-    lax.fori_loop(near, far, store_flux(stage, lo, hi), 0)
-
-    def section_two(t, carry):
-        l = layers + t
-        damp = damping(l, lo, hi)
-        for c, total in enumerate(change(stage, l, lo, hi)):
             value = 0.5 * state[c, l, lo:hi, :] + 0.5 * (
-                stage[c, l, lo:hi, :] + scale * total)
-            out[c, t] = value * damp if 1 <= c <= 3 else value
-        return carry
-
-    lax.fori_loop(0, layers, section_two, 0)
+                stage[c, l, lo:hi, :] + scale * whole(stage, c, l, lo, hi))
+            out[c, l - layers] = value * damp if 1 <= c <= 3 else value
+
+    each(layers, layers, section_two)
 
     for copy in x_sends + edges + corner_x + corner_z + max_copies:
         copy.wait_send()
@@ -284,7 +325,6 @@
 def per_device(n, conserved, solid_mask, penalty):
     _, layers, rows, width = conserved.shape
     tall = rows + 2 * EDGE
-    steps = n.bit_length() - 1
     dma = pltpu.SemaphoreType.DMA
     return pl.pallas_call(
         functools.partial(kernel, n),
@@ -299,13 +339,15 @@
             pltpu.VMEM((5, 3 * layers, tall, width), jnp.float32),
             pltpu.VMEM((3 * layers, tall, width), jnp.int32),
             pltpu.VMEM((4, 3 * layers, tall, width), jnp.float32),
+            pltpu.VMEM((4, 3 * layers, tall, width), jnp.float32),
             pltpu.VMEM((5, 3 * layers, tall, width), jnp.float32),
-            pltpu.VMEM((2 * steps + 3, 8, 128), jnp.float32),
+            pltpu.VMEM((5, 3 * layers, tall, width), jnp.float32),
+            pltpu.VMEM((n // 2 + 4, 8, 128), jnp.float32),
             dma((2,)),
             dma((12,)), dma((12,)),
             dma((12,)), dma((12,)),
             dma((8,)), dma((8,)),
-            dma((steps + 1,)), dma((steps + 1,)),
+            dma((n // 2 + 2,)), dma((n // 2 + 2,)),
         ],
         compiler_params=pltpu.CompilerParams(
             collective_id=0, has_side_effects=True, vmem_limit_bytes=40 * 1024 * 1024),

time: 48.2 us -> 36.5 us (0.76)
  Pallas kernels: 44.5 us -> 32.8 us
    pallas_call x1, Pallas kernels: 44.5 us -> 32.8 us  [per_device(): pl.pallas_call(functools.partial(kernel, n), out_shape=jax.ShapeDtypeStru...]
where the time goes in v2:
time: 36.5 us; the launch traced here: 36.3 us
  Pallas kernels  32.8 us (90%)
  local copies, waits for them, and re-layouts  3.51 us (10%)
    pallas_call x1, Pallas kernels, per_device(): pl.pallas_call(functools.partial(kernel, n), out_shape=jax.ShapeDtypeStru...  32.8 us
    unnamed x7, local copies, waits for them, and re-layouts  3.51 us

profile of v2, /device:TPU:0, one launch (start us, length us, event | category | flops | bytes accessed | tf_op | source)
XLA Modules:
  0.0 36.3 jit_solution(4073099829505204994)
XLA Ops:
  0.0 0.0 copy-start.2
  0.0 0.7 %copy-done.2 = f32[256]{0:T(256)S(1)} copy-done((f32[256]{0:T(256)S(1)}, f32[256]{0:T(256)}, u32[]{:S(2)}) %copy-start.2) | copy-done | bytes 1048
  0.7 0.0 copy-start
  0.7 1.1 %copy-done = f32[5,4,32,256]{3,2,1,0:T(8,128)S(1)} copy-done((f32[5,4,32,256]{3,2,1,0:T(8,128)S(1)}, f32[5,4,32,256]{3,2,1,0:T(8,128)}, u32[]{:S(2)}) %copy-start) | copy-done | bytes 655384
  1.8 0.0 copy-start.1
  1.8 0.9 %copy-done.1 = s32[4,32,256]{2,1,0:T(8,128)S(1)} copy-done((s32[4,32,256]{2,1,0:T(8,128)S(1)}, s32[4,32,256]{2,1,0:T(8,128)}, u32[]{:S(2)}) %copy-start.1) | copy-done | bytes 131096
  2.7 32.8 %shard_map.37 = f32[5,4,32,256]{3,2,1,0:T(8,128)S(1)} custom-call(f32[5,4,32,256]{3,2,1,0:T(8,128)S(1)} %copy-done, s32[4,32,256]{2,1,0:T(8,128)S(1)} %copy-done.1, f32[1,256]{1,0:T(1,128)S(1)} %bitcast.1), custom_call_target="tpu_custom_call" | custom-call | tf_op jit(solution)/shard_map/pallas_call | solution.py:329
  35.4 0.8 %copy.5 = f32[5,4,32,256]{3,2,1,0:T(8,128)} copy(f32[5,4,32,256]{3,2,1,0:T(8,128)S(1)} %shard_map.37) | data formatting | bytes 1310720
Async XLA Ops:
  0.0 0.7 %copy-start.2 = (f32[256]{0:T(256)S(1)}, f32[256]{0:T(256)}, u32[]{:S(2)}) copy-start(f32[256]{0:T(256)} %param.5) | copy-start | bytes 3076
  0.7 1.1 %copy-start = (f32[5,4,32,256]{3,2,1,0:T(8,128)S(1)}, f32[5,4,32,256]{3,2,1,0:T(8,128)}, u32[]{:S(2)}) copy-start(f32[5,4,32,256]{3,2,1,0:T(8,128)} %q_hbm.1) | copy-start | bytes 1966084
  1.8 0.9 %copy-start.1 = (s32[4,32,256]{2,1,0:T(8,128)S(1)}, s32[4,32,256]{2,1,0:T(8,128)}, u32[]{:S(2)}) copy-start(s32[4,32,256]{2,1,0:T(8,128)} %mask_hbm.1) | copy-start | bytes 393220

commit v3 on v2

--- a/solution.py
+++ b/solution.py
@@ -51,11 +51,11 @@
     )
 
 
-def kernel(n, q_hbm, mask_hbm, penalty, out, state, mask, fluxes, fluxes_two, stage, part, best,
+def kernel(n, q_own, mask_own, penalty, out, state, mask, fluxes, fluxes_two, stage, part, best,
            local_sem, sx, rx, sz, rz, sy, ry, sm, rm):
     i = lax.axis_index("gx")
     g = lax.axis_index("gy")
-    layers, rows, width = q_hbm.shape[1:]
+    layers, rows, width = q_own.shape[1:]
     lo, hi, tall = EDGE, EDGE + rows, rows + 2 * EDGE
     half = layers // 2
     parity = lax.rem(i, 2)
@@ -65,18 +65,30 @@
     z_from = lax.rem(i - 2 + 4 * parity + n, n)
     level = [lax.rem(i + 2 * m, n) for m in range(1, n // 2)]
 
-    local_q = pltpu.make_async_copy(
-        q_hbm, state.at[:, layers:2 * layers, lo:hi, :], local_sem.at[0])
-    local_m = pltpu.make_async_copy(
-        mask_hbm, mask.at[layers:2 * layers, lo:hi, :], local_sem.at[1])
-    local_q.start()
-    local_m.start()
-
     barrier = pltpu.get_barrier_semaphore()
     near_by = [{"gy": sibling}, {"gx": partner}, {"gx": partner, "gy": sibling}]
     others = near_by + [{"gx": j} for j in level]
     for where in others:
         pl.semaphore_signal(barrier, inc=1, device_id=where, device_id_type=MESH)
+    local_q = pltpu.make_async_copy(
+        q_own, state.at[:, layers:2 * layers, lo:hi, :], local_sem.at[0])
+    local_m = pltpu.make_async_copy(
+        mask_own, mask.at[layers:2 * layers, lo:hi, :], local_sem.at[1])
+    local_q.start()
+    local_m.start()
+
+    def speed_step(l, top):
+        rho, _, _, inverse, squares, pressure = primitives(
+            lambda c: q_own[c, l])
+        speed = jnp.sqrt(squares * inverse * inverse) + jnp.sqrt(
+            GAMMA_FULL * pressure * inverse)
+        for r in range(0, rows, 8):
+            for z in range(0, width, 128):
+                top = jnp.maximum(top, speed[r:r + 8, z:z + 128])
+        return top
+
+    best[0] = lax.fori_loop(0, layers, speed_step, jnp.zeros((8, 128), jnp.float32))
+
     pl.semaphore_wait(barrier, len(others))
 
     def remote(src, dst, send, recv, where):
@@ -88,17 +100,17 @@
     seen = (half - half * parity, half * parity)
     x_out, x_in = 2 * layers * parity, 2 * layers * (1 - parity)
     z_out = z_in = 2 * layers * parity
-    pieces = [(h, c) for h in range(2) for c in range(-1, 5)]
+    pieces = [(h, c) for h in range(2) for c in (0, 1, 2, 3, 4, -1)]
     x_sends, x_waits, z_sends, z_waits = [], [], [], []
     for k, (h, c) in enumerate(pieces):
         def x_copy(start, where):
             if c < 0:
                 return remote(
-                    mask_hbm.at[pl.ds(start, half)],
+                    mask_own.at[pl.ds(start, half)],
                     mask.at[pl.ds(where + start, half), lo:hi, :],
                     sx.at[k], rx.at[k], {"gx": partner})
             return remote(
-                q_hbm.at[c, pl.ds(start, half)],
+                q_own.at[c, pl.ds(start, half)],
                 state.at[c, pl.ds(where + start, half), lo:hi, :],
                 sx.at[k], rx.at[k], {"gx": partner})
 
@@ -122,18 +134,27 @@
             z_sends.append(z_copy(seen[h], x_in, z_out))
             z_waits.append(z_copy(seen[h], z_in, z_in))
 
+    def max_copy(k):
+        source = 0 if k < 3 else 4
+        return remote(best.at[source], best.at[k + 1 if k < 3 else k + 2],
+                      sm.at[k], rm.at[k], others[k])
+
+    max_copies = [max_copy(k) for k in range(len(others))]
+    for copy in max_copies[:3]:
+        copy.start()
+
     for copy in x_sends[:AHEAD]:
         copy.start()
 
     to_sibling = {"gy": sibling}
     edges = [
-        remote(q_hbm.at[:, :, 0:EDGE, :], state.at[:, layers:2 * layers, hi:tall, :],
+        remote(q_own.at[:, :, 0:EDGE, :], state.at[:, layers:2 * layers, hi:tall, :],
                sy.at[0], ry.at[0], to_sibling),
-        remote(q_hbm.at[:, :, rows - EDGE:rows, :], state.at[:, layers:2 * layers, 0:lo, :],
+        remote(q_own.at[:, :, rows - EDGE:rows, :], state.at[:, layers:2 * layers, 0:lo, :],
                sy.at[1], ry.at[1], to_sibling),
-        remote(mask_hbm.at[:, 0:EDGE, :], mask.at[layers:2 * layers, hi:tall, :],
+        remote(mask_own.at[:, 0:EDGE, :], mask.at[layers:2 * layers, hi:tall, :],
                sy.at[2], ry.at[2], to_sibling),
-        remote(mask_hbm.at[:, rows - EDGE:rows, :], mask.at[layers:2 * layers, 0:lo, :],
+        remote(mask_own.at[:, rows - EDGE:rows, :], mask.at[layers:2 * layers, 0:lo, :],
                sy.at[3], ry.at[3], to_sibling),
     ]
 
@@ -150,29 +171,6 @@
     corner_x = corner(x_in + seen[1], 6)
     for copy in edges:
         copy.start()
-    local_q.wait()
-
-    def speed_step(l, top):
-        rho, _, _, inverse, squares, pressure = primitives(
-            lambda c: state[c, layers + l, lo:hi, :])
-        speed = jnp.sqrt(squares * inverse * inverse) + jnp.sqrt(
-            GAMMA_FULL * pressure * inverse)
-        for r in range(0, rows, 8):
-            for z in range(0, width, 128):
-                top = jnp.maximum(top, speed[r:r + 8, z:z + 128])
-        return top
-
-    best[0] = lax.fori_loop(0, layers, speed_step, jnp.zeros((8, 128), jnp.float32))
-
-    def max_copy(k):
-        source = 0 if k < 3 else 4
-        return remote(best.at[source], best.at[k + 1 if k < 3 else k + 2],
-                      sm.at[k], rm.at[k], others[k])
-
-    max_copies = [max_copy(k) for k in range(len(others))]
-    for copy in max_copies[:3]:
-        copy.start()
-
     z_inner, z_outer = z_in + seen[0], z_in + seen[1]
     x_outer, x_inner = x_in + seen[0], x_in + seen[1]
     own_z = layers + half * parity
@@ -244,6 +242,11 @@
             z_sends[k].start()
         if k + AHEAD < len(pieces):
             x_sends[k + AHEAD].start()
+        if k == 0:
+            for copy in edges:
+                copy.wait_recv()
+            local_q.wait()
+            each(own_z, half, store_part(state, 0, tall))
         if k == 1:
             for copy in max_copies[:3]:
                 copy.wait_recv()
@@ -251,28 +254,24 @@
                 jnp.maximum(best[0], best[1]), jnp.maximum(best[2], best[3]))
             for copy in max_copies[3:]:
                 copy.start()
-            for copy in edges:
-                copy.wait_recv()
-            each(own_z, half, store_part(state, 0, tall))
+            each(own_x, half, store_part(state, 0, tall))
         if k == 2:
-            each(own_x, half, store_part(state, 0, tall))
-        if k == 3:
             each(layers, layers, store_flux(state, 0, tall))
         if k == 5:
             each(x_outer, half, store_flux(state, lo, hi))
-        if k == 7:
-            for h in range(6):
+        if k == 6:
+            for h in range(5):
                 z_waits[h].wait_recv()
             for copy in corner_z:
                 copy.start()
-            for copy in max_copies[3:]:
-                copy.wait_recv()
-        if k == 8:
+        if k == 7:
             for copy in corner_z:
                 copy.wait_recv()
             each(z_inner, half, store_flux(state, 0, tall))
             each(z_inner, half, store_part(state, lo, hi))
-        if k == 9:
+        if k == 8:
+            for copy in max_copies[3:]:
+                copy.wait_recv()
             local_m.wait()
             top = best[4]
             for m in range(len(level)):
@@ -280,15 +279,17 @@
             top = jnp.max(jnp.max(top, axis=1, keepdims=True), axis=0, keepdims=True)
             time_step = COURANT / top
             each(own_z, half, section_one(0, tall, time_step))
-        if k == 10:
+        if k == 9:
             each(own_z, half, store_part(stage, lo, hi))
             each(own_z, half, store_flux(stage, lo, hi))
-
-    for copy in corner_x:
-        copy.start()
-    each(x_inner, half, store_flux(state, lo, hi))
+        if k == 10:
+            for copy in corner_x:
+                copy.start()
+            each(x_inner, half, store_flux(state, lo, hi))
+
+    z_waits[5].wait_recv()
     each(own_x, half, section_one(lo, hi, time_step))
-    for k in range(7, 12):
+    for k in range(6, 11):
         z_waits[k].wait_recv()
     each(z_outer, half, store_flux(state, lo, hi))
     each(z_inner, half, section_one(lo, hi, time_step))
@@ -330,8 +331,8 @@
         functools.partial(kernel, n),
         out_shape=jax.ShapeDtypeStruct(conserved.shape, jnp.float32),
         in_specs=[
-            pl.BlockSpec(memory_space=pl.ANY),
-            pl.BlockSpec(memory_space=pl.ANY),
+            pl.BlockSpec(memory_space=pltpu.VMEM),
+            pl.BlockSpec(memory_space=pltpu.VMEM),
             pl.BlockSpec(memory_space=pltpu.VMEM),
         ],
         out_specs=pl.BlockSpec(memory_space=pltpu.VMEM),

time: 36.5 us -> 33.8 us (0.926)
  Pallas kernels: 32.8 us -> 30.1 us
    pallas_call x1, Pallas kernels: 32.8 us -> 30.1 us  [per_device(): pl.pallas_call(functools.partial(kernel, n), out_shape=jax.ShapeDtypeStru...]
where the time goes in v3:
time: 33.8 us; the launch traced here: 33.6 us
  Pallas kernels  30.1 us (89%)
  local copies, waits for them, and re-layouts  3.51 us (10%)
    pallas_call x1, Pallas kernels, per_device(): pl.pallas_call(functools.partial(kernel, n), out_shape=jax.ShapeDtypeStru...  30.1 us
    unnamed x7, local copies, waits for them, and re-layouts  3.51 us

profile of v3, /device:TPU:0, one launch (start us, length us, event | category | flops | bytes accessed | tf_op | source)
XLA Modules:
  0.0 33.6 jit_solution(2221898346827792429)
XLA Ops:
  0.0 0.0 copy-start.2
  0.0 0.7 %copy-done.2 = f32[256]{0:T(256)S(1)} copy-done((f32[256]{0:T(256)S(1)}, f32[256]{0:T(256)}, u32[]{:S(2)}) %copy-start.2) | copy-done | bytes 1048
  0.7 0.0 copy-start
  0.7 1.1 %copy-done = f32[5,4,32,256]{3,2,1,0:T(8,128)S(1)} copy-done((f32[5,4,32,256]{3,2,1,0:T(8,128)S(1)}, f32[5,4,32,256]{3,2,1,0:T(8,128)}, u32[]{:S(2)}) %copy-start) | copy-done | bytes 655384
  1.8 0.0 copy-start.1
  1.8 0.9 %copy-done.1 = s32[4,32,256]{2,1,0:T(8,128)S(1)} copy-done((s32[4,32,256]{2,1,0:T(8,128)S(1)}, s32[4,32,256]{2,1,0:T(8,128)}, u32[]{:S(2)}) %copy-start.1) | copy-done | bytes 131096
  2.7 30.1 %shard_map.37 = f32[5,4,32,256]{3,2,1,0:T(8,128)S(1)} custom-call(f32[5,4,32,256]{3,2,1,0:T(8,128)S(1)} %copy-done, s32[4,32,256]{2,1,0:T(8,128)S(1)} %copy-done.1, f32[1,256]{1,0:T(1,128)S(1)} %bitcast.1), custom_call_target="tpu_custom_call" | custom-call | tf_op jit(solution)/shard_map/pallas_call | solution.py:330
  32.8 0.8 %copy.5 = f32[5,4,32,256]{3,2,1,0:T(8,128)} copy(f32[5,4,32,256]{3,2,1,0:T(8,128)S(1)} %shard_map.37) | data formatting | bytes 1310720
Async XLA Ops:
  0.0 0.7 %copy-start.2 = (f32[256]{0:T(256)S(1)}, f32[256]{0:T(256)}, u32[]{:S(2)}) copy-start(f32[256]{0:T(256)} %param.5) | copy-start | bytes 3076
  0.7 1.1 %copy-start = (f32[5,4,32,256]{3,2,1,0:T(8,128)S(1)}, f32[5,4,32,256]{3,2,1,0:T(8,128)}, u32[]{:S(2)}) copy-start(f32[5,4,32,256]{3,2,1,0:T(8,128)} %q_own.1) | copy-start | bytes 1966084
  1.8 0.9 %copy-start.1 = (s32[4,32,256]{2,1,0:T(8,128)S(1)}, s32[4,32,256]{2,1,0:T(8,128)}, u32[]{:S(2)}) copy-start(s32[4,32,256]{2,1,0:T(8,128)} %mask_own.1) | copy-start | bytes 393220

commit v4 on v2

--- a/solution.py
+++ b/solution.py
@@ -13,7 +13,8 @@
 VISCOSITY = 0.05
 MESH = pl.DeviceIdType.MESH
 EDGE = 8
-AHEAD = 4
+AHEAD = 8
+FIRST = 4
 
 
 def rolled(value, shift, axis):
@@ -51,11 +52,11 @@
     )
 
 
-def kernel(n, q_hbm, mask_hbm, penalty, out, state, mask, fluxes, fluxes_two, stage, part, best,
+def kernel(n, q_own, mask_own, penalty_own, out, state, mask, penalty, fluxes, fluxes_two, stage, part, best,
            local_sem, sx, rx, sz, rz, sy, ry, sm, rm):
     i = lax.axis_index("gx")
     g = lax.axis_index("gy")
-    layers, rows, width = q_hbm.shape[1:]
+    layers, rows, width = q_own.shape[1:]
     lo, hi, tall = EDGE, EDGE + rows, rows + 2 * EDGE
     half = layers // 2
     parity = lax.rem(i, 2)
@@ -66,11 +67,13 @@
     level = [lax.rem(i + 2 * m, n) for m in range(1, n // 2)]
 
     local_q = pltpu.make_async_copy(
-        q_hbm, state.at[:, layers:2 * layers, lo:hi, :], local_sem.at[0])
+        q_own, state.at[:, layers:2 * layers, lo:hi, :], local_sem.at[0])
     local_m = pltpu.make_async_copy(
-        mask_hbm, mask.at[layers:2 * layers, lo:hi, :], local_sem.at[1])
+        mask_own, mask.at[layers:2 * layers, lo:hi, :], local_sem.at[1])
     local_q.start()
     local_m.start()
+    local_p = pltpu.make_async_copy(penalty_own, penalty, local_sem.at[2])
+    local_p.start()
 
     barrier = pltpu.get_barrier_semaphore()
     near_by = [{"gy": sibling}, {"gx": partner}, {"gx": partner, "gy": sibling}]
@@ -88,52 +91,52 @@
     seen = (half - half * parity, half * parity)
     x_out, x_in = 2 * layers * parity, 2 * layers * (1 - parity)
     z_out = z_in = 2 * layers * parity
-    pieces = [(h, c) for h in range(2) for c in range(-1, 5)]
+    pieces = [(h, c, d) for h in range(2) for c in (0, 1, 2, 3, 4, -1) for d in range(half)]
     x_sends, x_waits, z_sends, z_waits = [], [], [], []
-    for k, (h, c) in enumerate(pieces):
+    for k, (h, c, d) in enumerate(pieces):
         def x_copy(start, where):
             if c < 0:
                 return remote(
-                    mask_hbm.at[pl.ds(start, half)],
-                    mask.at[pl.ds(where + start, half), lo:hi, :],
+                    mask_own.at[pl.ds(start, 1)],
+                    mask.at[pl.ds(where + start, 1), lo:hi, :],
                     sx.at[k], rx.at[k], {"gx": partner})
             return remote(
-                q_hbm.at[c, pl.ds(start, half)],
-                state.at[c, pl.ds(where + start, half), lo:hi, :],
+                q_own.at[c, pl.ds(start, 1)],
+                state.at[c, pl.ds(where + start, 1), lo:hi, :],
                 sx.at[k], rx.at[k], {"gx": partner})
 
         def z_copy(start, source, target):
             if c < 0:
                 return remote(
-                    mask.at[pl.ds(source + start, half), lo:hi, :],
-                    mask.at[pl.ds(target + start, half), lo:hi, :],
+                    mask.at[pl.ds(source + start, 1), lo:hi, :],
+                    mask.at[pl.ds(target + start, 1), lo:hi, :],
                     sz.at[k], rz.at[k], {"gx": z_to})
             return remote(
-                state.at[c, pl.ds(source + start, half), lo:hi, :],
-                state.at[c, pl.ds(target + start, half), lo:hi, :],
+                state.at[c, pl.ds(source + start, 1), lo:hi, :],
+                state.at[c, pl.ds(target + start, 1), lo:hi, :],
                 sz.at[k], rz.at[k], {"gx": z_to})
 
-        x_sends.append(x_copy(own[h], x_out))
-        x_waits.append(x_copy(seen[h], x_in))
+        x_sends.append(x_copy(own[h] + d, x_out))
+        x_waits.append(x_copy(seen[h] + d, x_in))
         if c < 0 and h == 1:
             z_sends.append(None)
             z_waits.append(None)
         else:
-            z_sends.append(z_copy(seen[h], x_in, z_out))
-            z_waits.append(z_copy(seen[h], z_in, z_in))
-
-    for copy in x_sends[:AHEAD]:
+            z_sends.append(z_copy(seen[h] + d, x_in, z_out))
+            z_waits.append(z_copy(seen[h] + d, z_in, z_in))
+
+    for copy in x_sends[:FIRST]:
         copy.start()
 
     to_sibling = {"gy": sibling}
     edges = [
-        remote(q_hbm.at[:, :, 0:EDGE, :], state.at[:, layers:2 * layers, hi:tall, :],
+        remote(q_own.at[:, :, 0:EDGE, :], state.at[:, layers:2 * layers, hi:tall, :],
                sy.at[0], ry.at[0], to_sibling),
-        remote(q_hbm.at[:, :, rows - EDGE:rows, :], state.at[:, layers:2 * layers, 0:lo, :],
+        remote(q_own.at[:, :, rows - EDGE:rows, :], state.at[:, layers:2 * layers, 0:lo, :],
                sy.at[1], ry.at[1], to_sibling),
-        remote(mask_hbm.at[:, 0:EDGE, :], mask.at[layers:2 * layers, hi:tall, :],
+        remote(mask_own.at[:, 0:EDGE, :], mask.at[layers:2 * layers, hi:tall, :],
                sy.at[2], ry.at[2], to_sibling),
-        remote(mask_hbm.at[:, rows - EDGE:rows, :], mask.at[layers:2 * layers, 0:lo, :],
+        remote(mask_own.at[:, rows - EDGE:rows, :], mask.at[layers:2 * layers, 0:lo, :],
                sy.at[3], ry.at[3], to_sibling),
     ]
 
@@ -150,7 +153,6 @@
     corner_x = corner(x_in + seen[1], 6)
     for copy in edges:
         copy.start()
-    local_q.wait()
 
     def speed_step(l, top):
         rho, _, _, inverse, squares, pressure = primitives(
@@ -162,6 +164,7 @@
                 top = jnp.maximum(top, speed[r:r + 8, z:z + 128])
         return top
 
+    local_q.wait()
     best[0] = lax.fori_loop(0, layers, speed_step, jnp.zeros((8, 128), jnp.float32))
 
     def max_copy(k):
@@ -171,6 +174,9 @@
 
     max_copies = [max_copy(k) for k in range(len(others))]
     for copy in max_copies[:3]:
+        copy.start()
+
+    for copy in x_sends[FIRST:AHEAD]:
         copy.start()
 
     z_inner, z_outer = z_in + seen[0], z_in + seen[1]
@@ -244,51 +250,55 @@
             z_sends[k].start()
         if k + AHEAD < len(pieces):
             x_sends[k + AHEAD].start()
-        if k == 1:
+        if k == half * 0 + half - 1:
+            for copy in edges:
+                copy.wait_recv()
+            each(own_z, half, store_part(state, 0, tall))
+        if k == half * 1 + half - 1:
             for copy in max_copies[:3]:
                 copy.wait_recv()
             best[4] = jnp.maximum(
                 jnp.maximum(best[0], best[1]), jnp.maximum(best[2], best[3]))
             for copy in max_copies[3:]:
                 copy.start()
-            for copy in edges:
-                copy.wait_recv()
-            each(own_z, half, store_part(state, 0, tall))
-        if k == 2:
             each(own_x, half, store_part(state, 0, tall))
-        if k == 3:
+        if k == half * 2 + half - 1:
             each(layers, layers, store_flux(state, 0, tall))
-        if k == 5:
+        if k == half * 5 + half - 1:
             each(x_outer, half, store_flux(state, lo, hi))
-        if k == 7:
-            for h in range(6):
+        if k == half * 6 + half - 1:
+            for h in range(5 * half):
                 z_waits[h].wait_recv()
             for copy in corner_z:
                 copy.start()
-            for copy in max_copies[3:]:
-                copy.wait_recv()
-        if k == 8:
+        if k == half * 7 + half - 1:
             for copy in corner_z:
                 copy.wait_recv()
             each(z_inner, half, store_flux(state, 0, tall))
             each(z_inner, half, store_part(state, lo, hi))
-        if k == 9:
+        if k == half * 8 + half - 1:
+            for copy in max_copies[3:]:
+                copy.wait_recv()
             local_m.wait()
+            local_p.wait()
             top = best[4]
             for m in range(len(level)):
                 top = jnp.maximum(top, best[5 + m])
             top = jnp.max(jnp.max(top, axis=1, keepdims=True), axis=0, keepdims=True)
             time_step = COURANT / top
             each(own_z, half, section_one(0, tall, time_step))
-        if k == 10:
+        if k == half * 9 + half - 1:
             each(own_z, half, store_part(stage, lo, hi))
             each(own_z, half, store_flux(stage, lo, hi))
-
-    for copy in corner_x:
-        copy.start()
-    each(x_inner, half, store_flux(state, lo, hi))
+        if k == half * 10 + half - 1:
+            for copy in corner_x:
+                copy.start()
+            each(x_inner, half, store_flux(state, lo, hi))
+
+    for h in range(5 * half, 6 * half):
+        z_waits[h].wait_recv()
     each(own_x, half, section_one(lo, hi, time_step))
-    for k in range(7, 12):
+    for k in range(6 * half, 11 * half):
         z_waits[k].wait_recv()
     each(z_outer, half, store_flux(state, lo, hi))
     each(z_inner, half, section_one(lo, hi, time_step))
@@ -328,29 +338,30 @@
     dma = pltpu.SemaphoreType.DMA
     return pl.pallas_call(
         functools.partial(kernel, n),
-        out_shape=jax.ShapeDtypeStruct(conserved.shape, jnp.float32),
+        out_shape=pltpu.VMEM(conserved.shape, jnp.float32),
         in_specs=[
-            pl.BlockSpec(memory_space=pl.ANY),
-            pl.BlockSpec(memory_space=pl.ANY),
-            pl.BlockSpec(memory_space=pltpu.VMEM),
+            pl.BlockSpec(memory_space=pltpu.HBM),
+            pl.BlockSpec(memory_space=pltpu.HBM),
+            pl.BlockSpec(memory_space=pltpu.HBM),
         ],
         out_specs=pl.BlockSpec(memory_space=pltpu.VMEM),
         scratch_shapes=[
             pltpu.VMEM((5, 3 * layers, tall, width), jnp.float32),
             pltpu.VMEM((3 * layers, tall, width), jnp.int32),
+            pltpu.VMEM((1, width), jnp.float32),
             pltpu.VMEM((4, 3 * layers, tall, width), jnp.float32),
             pltpu.VMEM((4, 3 * layers, tall, width), jnp.float32),
             pltpu.VMEM((5, 3 * layers, tall, width), jnp.float32),
             pltpu.VMEM((5, 3 * layers, tall, width), jnp.float32),
             pltpu.VMEM((n // 2 + 4, 8, 128), jnp.float32),
-            dma((2,)),
-            dma((12,)), dma((12,)),
-            dma((12,)), dma((12,)),
+            dma((3,)),
+            dma((6 * layers,)), dma((6 * layers,)),
+            dma((6 * layers,)), dma((6 * layers,)),
             dma((8,)), dma((8,)),
             dma((n // 2 + 2,)), dma((n // 2 + 2,)),
         ],
         compiler_params=pltpu.CompilerParams(
-            collective_id=0, has_side_effects=True, vmem_limit_bytes=40 * 1024 * 1024),
+            collective_id=0, has_side_effects=True, vmem_limit_bytes=63500 * 1024),
     )(conserved, solid_mask, penalty.reshape(1, width))
 
 

time: 36.5 us -> 31.2 us (0.85)
  local copies, waits for them, and re-layouts: 3.51 us -> 0.84 us
  Pallas kernels: 32.8 us -> 30.2 us
    unnamed x7 -> x1, local copies, waits for them, and re-layouts: 3.51 us -> 0.84 us
    pallas_call x1, Pallas kernels: 32.8 us -> 30.2 us  [per_device(): pl.pallas_call(functools.partial(kernel, n), out_shape=pltpu.VMEM(conserv...]
where the time goes in v4:
time: 31.2 us; the launch traced here: 31 us
  Pallas kernels  30.2 us (97%)
  local copies, waits for them, and re-layouts  0.84 us (3%)
    pallas_call x1, Pallas kernels, per_device(): pl.pallas_call(functools.partial(kernel, n), out_shape=pltpu.VMEM(conserv...  30.2 us
    unnamed x1, local copies, waits for them, and re-layouts  0.84 us

profile of v4, /device:TPU:0, one launch (start us, length us, event | category | flops | bytes accessed | tf_op | source)
XLA Modules:
  0.0 31.0 jit_solution(3588783661909974410)
XLA Ops:
  0.0 30.2 %shard_map.37 = f32[5,4,32,256]{3,2,1,0:T(8,128)S(1)} custom-call(f32[5,4,32,256]{3,2,1,0:T(8,128)} %q_own.1, s32[4,32,256]{2,1,0:T(8,128)} %mask_own.1, f32[1,256]{1,0:T(1,128)} %bitcast.1), custom_call_target="tpu_custom_call" | custom-call | tf_op jit(solution)/shard_map/pallas_call | solution.py:339
  30.2 0.8 %copy.5 = f32[5,4,32,256]{3,2,1,0:T(8,128)} copy(f32[5,4,32,256]{3,2,1,0:T(8,128)S(1)} %shard_map.37) | data formatting | bytes 1310720
